TPU v7x, 32 devices: a whole 2x2x4 slice. The times are simulated.
32 devices in a mesh: fsdp: 2 (over y), uly: 4 (over x, core), blk: 4 (over z).
Axes of the slice: x: 2, y: 2, z: 4, core: 2. Of those that a mesh axis runs over, the one named last changes fastest.
Arguments:
- latents: bfloat16 [2, 3072, 3072], P('fsdp', ('uly', 'blk')), may hold values from -40 to 40
- sampler_noise: bfloat16 [2, 3072, 3072], P('fsdp', ('uly', 'blk')), may hold values from -6 to 6
- query_key_value_weight: bfloat16 [3, 3072, 1536], P(None, 'fsdp', 'uly'), may hold values from -0.375 to 0.375
- output_weight: bfloat16 [3072, 1536], P('fsdp', 'uly'), may hold values from -0.15625 to 0.15625
- adapter_down_map: bfloat16 [64, 1536], P(None, 'uly'), may hold values from -0.15625 to 0.15625
- adapter_up_map: bfloat16 [64, 3072], replicated, may hold values from -0.75 to 0.75
- valid_token_count: int32 [2], P('fsdp'), may hold values from 1536 to 3072
- advantage: float32 [2], P('fsdp'), may hold values from -3 to 3
- timestep_index: int32 [1], replicated, may hold values from 1 to 15
Outputs:
- next_latents: bfloat16 [2, 3072, 3072], P('fsdp', ('uly', 'blk'))
- log_ratio: float32 [2], P('fsdp')
- grad_down: float32 [64, 1536], P(None, 'uly')
- grad_up: float32 [64, 3072], replicated
All inputs are finite; a program needn't handle non-finite values.
Results may differ from a plain program's by a relative error of at most 0.0055.
The roundings to bfloat16 on the way count: a program that leaves them out, or rounds other values in their place, can miss the bound.
Values may be sent and summed in bfloat16 or wider, within the bound.
A program may use at most 128 MiB of HBM per device.

v0:
```python
import math

import jax
import jax.numpy as jnp
from jax import lax
from jax.sharding import PartitionSpec as P

HEAD_SIZE = 128
STEPS = 16


noise_level = 0.7
loss_scale = 4194304.0
rms_eps = 1e-06


def shards(
    latents,
    sampler_noise,
    query_key_value_weight,
    output_weight,
    adapter_down_map,
    adapter_up_map,
    valid_token_count,
    advantage,
    timestep_index,
):
    current = latents[0].astype(jnp.float32)
    rows = current.shape[0]
    width = current.shape[1]
    normed = (current * lax.rsqrt(jnp.mean(current * current, -1, keepdims=True) + rms_eps)).astype(
        jnp.bfloat16
    )
    gathered = lax.all_gather(normed, "uly", axis=0, tiled=True)
    projected = jnp.einsum(
        "td,kdh->kth",
        gathered,
        lax.all_gather(query_key_value_weight, "fsdp", axis=1, tiled=True),
        preferred_element_type=jnp.float32,
    ).astype(jnp.bfloat16)
    query_rows = projected[0]
    key_rows, value_rows = (
        lax.all_gather(projected[1], "blk", axis=0, tiled=True),
        lax.all_gather(projected[2], "blk", axis=0, tiled=True),
    )
    uly_count = lax.axis_size("uly")
    blk_count = lax.axis_size("blk")
    uly_id = lax.axis_index("uly")
    blk_id = lax.axis_index("blk")
    limit = valid_token_count[0]
    group_rows = uly_count * rows
    key_index = jnp.arange(key_rows.shape[0], dtype=jnp.int32)
    key_pos = (
        key_index % group_rows // rows * blk_count + key_index // group_rows
    ) * rows + key_index % rows
    key_ok = (key_pos < limit)[None, None, :]
    heads_here = query_rows.shape[1] // HEAD_SIZE
    query_split = query_rows.reshape(query_rows.shape[0], heads_here, HEAD_SIZE)
    key_split = key_rows.reshape(key_rows.shape[0], heads_here, HEAD_SIZE)
    value_split = value_rows.reshape(value_rows.shape[0], heads_here, HEAD_SIZE)
    scores = jnp.einsum(
        "qhd,khd->hqk", query_split, key_split, preferred_element_type=jnp.float32
    ) * (1.0 / math.sqrt(HEAD_SIZE))
    masked = jnp.where(key_ok, scores, -1e30)
    row_max = jnp.max(masked, -1, keepdims=True)
    exp_terms = jnp.where(key_ok, jnp.exp(masked - row_max), 0.0)
    weights = (exp_terms / jnp.sum(exp_terms, -1, keepdims=True)).astype(jnp.bfloat16)
    attention_output = jnp.einsum(
        "hqk,khd->qhd", weights, value_split, preferred_element_type=jnp.float32
    )
    attention_output = attention_output.astype(jnp.bfloat16).reshape(
        query_rows.shape[0], heads_here * HEAD_SIZE
    )
    weight_cols = lax.all_gather(output_weight, "fsdp", axis=0, tiled=True)
    contract_product = (((1,), (1,)), ((), ()))
    own_heads = lax.all_to_all(attention_output, "uly", split_axis=0, concat_axis=1, tiled=True)
    weight_full, down_full = (
        lax.all_gather(weight_cols, "uly", axis=1, tiled=True),
        lax.all_gather(adapter_down_map, "uly", axis=1, tiled=True),
    )
    velocity = lax.dot_general(
        own_heads, weight_full, contract_product, preferred_element_type=jnp.float32
    )
    narrow_projection = lax.dot_general(
        own_heads, down_full, contract_product, preferred_element_type=jnp.float32
    ).astype(jnp.bfloat16)
    adapter_result = jnp.dot(narrow_projection, adapter_up_map, preferred_element_type=jnp.float32)
    step_float = timestep_index[0].astype(jnp.float32)
    time_now = 1.0 - step_float / STEPS
    step_size = 1.0 / STEPS
    noise_std = noise_level * jnp.sqrt(time_now / (1.0 - time_now))
    drift_gain = 1.0 + noise_level**2 / 2.0
    ratio_gain = jnp.sqrt(step_size) * drift_gain / noise_std
    noise_f = sampler_noise[0].astype(jnp.float32)
    moved = current - step_size * (
        drift_gain * velocity + noise_level**2 * current / (2.0 * (1.0 - time_now))
    )
    next_latents = (moved + noise_std * jnp.sqrt(step_size) * noise_f).astype(jnp.bfloat16)[None]
    standard = noise_f + ratio_gain * adapter_result
    tok_pos = (uly_id * blk_count + blk_id) * rows + jnp.arange(rows, dtype=jnp.int32)
    tok_ok = (tok_pos < limit)[:, None]
    valid_len = limit.astype(jnp.float32)
    partial_log = jnp.sum(jnp.where(tok_ok, noise_f * noise_f - standard * standard, 0.0)) / (
        2.0 * valid_len * width
    )
    log_ratio = lax.psum(partial_log, ("uly", "blk"))
    coef = (
        loss_scale
        * advantage[0]
        * jnp.exp(log_ratio)
        * ratio_gain
        / (lax.axis_size("fsdp") * valid_len * width)
    )
    delta_gradient = (jnp.where(tok_ok, standard, 0.0) * coef).astype(jnp.bfloat16)
    first_axis = (((0,), (0,)), ((), ()))
    up_part = lax.dot_general(
        narrow_projection, delta_gradient, first_axis, preferred_element_type=jnp.float32
    )
    narrow_gradient = lax.dot_general(
        delta_gradient, adapter_up_map, contract_product, preferred_element_type=jnp.float32
    ).astype(jnp.bfloat16)
    down_part = lax.dot_general(
        narrow_gradient, own_heads, first_axis, preferred_element_type=jnp.float32
    )
    grad_up, down_total = lax.psum((up_part, down_part), ("fsdp", "uly", "blk"))
    local_columns = adapter_down_map.shape[1]
    grad_down = lax.dynamic_slice_in_dim(down_total, uly_id * local_columns, local_columns, 1)
    return (next_latents, jnp.reshape(log_ratio, (1,)), grad_down, grad_up)


def solution(mesh):
    placed = (
        P("fsdp", ("uly", "blk"), None),
        P("fsdp", ("uly", "blk"), None),
        P(None, "fsdp", "uly"),
        P("fsdp", "uly"),
        P(None, "uly"),
        P(),
        P("fsdp"),
        P("fsdp"),
        P(),
    )
    return jax.shard_map(
        shards,
        mesh=mesh,
        in_specs=placed,
        out_specs=(P("fsdp", ("uly", "blk"), None), P("fsdp"), P(None, "uly"), P()),
        check_vma=False,
    )
```

profile of v0, /device:TPU:0, one launch (start us, length us, event | category | flops | bytes accessed | tf_op | source)
XLA Modules:
  0.0 536.7 jit_solution(5400782425522006740)
XLA Ops:
  7.2 0.0 copy-start
  7.2 0.0 all-gather.11.cloned.1.call-start
  7.2 6.1 %copy.16 = bf16[3,1536,384]{1,2,0:T(8,128)(2,1)} copy(bf16[3,1536,384]{2,1,0:T(8,128)(2,1)} %param.11) | data formatting | bytes 7077888 | tf_op args[2]
  13.4 0.0 copy-start.1
  13.4 0.0 all-gather.11.cloned.1.call-update
  13.4 0.0 all-gather.9.cloned.1.call-start
  13.4 1.2 copy-done.1
  14.6 0.3 fusion.19
  15.0 1.3 fusion.20
  16.3 0.0 all-gather.9.cloned.1.call-update
  16.3 0.0 all-gather.19.cloned.1.call-start
  16.4 89.1 %all-gather.11.cloned.1.call-done = bf16[3,3072,384]{1,2,0:T(8,128)(2,1)} async-done(((bf16[3,1536,384]{1,2,0:T(8,128)(2,1)}), bf16[3,3072,384]{1,2,0:T(8,128)(2,1)}) %all-gather.11.cloned.1.call-update) | async-done | bytes 7077904 | tf_op jit(solution)/shard_map/all_gather | solution.py:38
  105.5 39.6 %all-gather.9.cloned.1.call-done = bf16[768,3072]{1,0:T(8,128)(2,1)} async-done(((bf16[192,3072]{1,0:T(8,128)(2,1)}), bf16[768,3072]{1,0:T(8,128)(2,1)}) %all-gather.9.cloned.1.call-update) | async-done | bytes 4718608 | tf_op jit(solution)/shard_map/all_gather | solution.py:34
  145.1 9.3 %convert_bitcast_fusion = bf16[3,768,384]{1,2,0:T(8,128)(2,1)S(1)} fusion(bf16[3,3072,384]{1,2,0:T(8,128)(2,1)} %all-gather.11.cloned.1.call-done, bf16[768,3072]{1,0:T(8,128)(2,1)} %all-gather.9.cloned.1.call-done), kind=kOutput, calls=%fused_computation.33 | convolution fusion | flops 5436702720 | bytes 13565952 | tf_op jit(solution)/shard_map/td,kdh->kth/dot_general | solution.py:35
  154.5 1.1 fusion.53
  155.6 0.0 all-gather.19.cloned.1.call-update
  155.6 0.0 all-gather.17.cloned.1.call-start
  155.7 0.5 all-gather.17.cloned.1.call-update
  156.2 0.0 all-gather.13.cloned.1.call-start
  156.2 0.5 all-gather.13.cloned.1.call-update
  157.5 48.8 %all-gather.19.cloned.1.call-done = bf16[1,3072,384]{1,2,0:T(8,128)(2,1)} async-done(((bf16[1,768,384]{1,2,0:T(8,128)(2,1)}), bf16[1,3072,384]{1,2,0:T(8,128)(2,1)}) %all-gather.19.cloned.1.call-update) | async-done | bytes 2359312 | tf_op jit(solution)/shard_map/all_gather | solution.py:43
  206.2 16.2 %fusion.54 = (f32[3,768]{1,0:T(4,128)S(1)}, f32[3,768,3072]{2,1,0:T(8,128)}) fusion(pred[3072]{0:T(1024)(128)(4,1)S(1)} %fusion.47, bf16[768,3,128]{0,2,1:T(8,128)(2,1)S(1)} %bitcast.55, bf16[3072,3,128]{0,2,1:T(8,128)(2,1)} %bitcast.56), kind=kOutput, calls=%fused_computation.75 | convolution fusion | flops 1847331840 | bytes 31272960 | tf_op jit(solution)/shard_map/sub | solution.py:66
  222.5 35.1 %all-gather.17.cloned.1.call-done = bf16[1,3072,384]{1,2,0:T(8,128)(2,1)} async-done(((bf16[1,768,384]{1,2,0:T(8,128)(2,1)}), bf16[1,3072,384]{1,2,0:T(8,128)(2,1)}) %all-gather.17.cloned.1.call-update) | async-done | bytes 2359312 | tf_op jit(solution)/shard_map/all_gather | solution.py:44
  257.5 13.2 %fusion.25 = bf16[768,3,128]{0,2,1:T(8,128)(2,1)S(1)} fusion(bf16[3072,3,128]{0,2,1:T(8,128)(2,1)} %bitcast.57, f32[3,768,3072]{2,1,0:T(8,128)} %get-tuple-element.10, f32[3,768]{1,0:T(4,128)S(1)} %get-tuple-element.9), kind=kOutput, calls=%fused_computation.35 | convolution fusion | flops 1826390016 | bytes 31269888 | tf_op jit(solution)/shard_map/hqk,khd->qhd/dot_general | solution.py:68
  270.7 0.0 copy-start.4
  270.7 0.7 reshape.95
  271.4 1.4 copy.23
  272.9 3.5 all-to-all-start
  276.3 0.0 all-reduce.3.cloned.1.call-start
  277.8 0.0 copy-done.4
  277.8 9.9 %all_gather.27 = bf16[64,1536]{1,0:T(8,128)(2,1)S(1)} all-gather(bf16[64,384]{1,0:T(8,128)(2,1)S(1)} %copy-done.4), channel_id=1, replica_groups=mesh['fsdp'=2,'uly'=4,'blk'=4] {'uly'}, dimensions={1}, use_global_device_ids=true | all-gather | bytes 245760 | tf_op jit(solution)/shard_map/all_gather | solution.py:79
  287.7 0.0 all-to-all-done
  287.7 0.1 copy.24
  287.8 0.3 convolution_convert_fusion.1
  288.1 0.0 copy-done
  288.1 2.8 fusion.18
  291.6 30.2 %psum.21 = f32[]{:T(128)} all-reduce(f32[]{:T(128)S(6)} %div.64), channel_id=1, replica_groups=mesh['fsdp'=2,'uly'=4,'blk'=4] {'uly','blk'}, use_global_device_ids=true, to_apply=%region_4.5 | all-reduce | flops 1 | bytes 8 | tf_op jit(solution)/shard_map/psum | solution.py:106
  322.5 1.3 fusion.52
  323.9 1.7 fusion.26
  325.5 0.0 copy-start.2
  325.5 0.0 all-reduce.3.cloned.1.call-update
  325.6 0.0 all-gather.15.cloned.1.call-start
  325.6 0.0 all-gather.13.cloned.1.call-done
  325.6 0.7 all-gather.15.cloned.1.call-update
  326.3 129.6 %all-reduce.3.cloned.1.call-done = (f32[64,1536]{1,0:T(8,128)}, f32[64,3072]{1,0:T(8,128)}) async-done(((f32[64,1536]{1,0:T(8,128)}, f32[64,3072]{1,0:T(8,128)}), (f32[64,1536]{1,0:T(8,128)}, f32[64,3072]{1,0:T(8,128)})) %all-reduce.3.cloned.1.call-update) | async-done | bytes 1179664 | tf_op jit(solution)/shard_map/psum | solution.py:125
  455.9 1.5 constant_dynamic-slice_fusion
  457.5 0.0 copy-start.3
  457.5 63.2 %all-gather.15.cloned.1.call-done = bf16[3072,1536]{1,0:T(8,128)(2,1)} async-done(((bf16[3072,384]{1,0:T(8,128)(2,1)}), bf16[3072,1536]{1,0:T(8,128)(2,1)}) %all-gather.15.cloned.1.call-update) | async-done | bytes 9437200 | tf_op jit(solution)/shard_map/all_gather | solution.py:78
  520.7 0.0 copy-done.2
  520.7 8.3 %fusion.13 = bf16[1,192,3072]{2,1,0:T(8,128)(2,1)} fusion(bf16[192,1536]{1,0:T(8,128)(2,1)S(1)} %bitcast.53, bf16[3072,1536]{1,0:T(8,128)(2,1)} %all-gather.15.cloned.1.call-done, bf16[1,192,3072]{2,1,0:T(8,128)(2,1)} %param.10, bf16[1,192,3072]{2,1,0:T(8,128)(2,1)S(1)} %copy-done.2, f32[]{:T(128)S(6)} %mul.119, f32[]{:T(128)S(6)} %mul.116), kind=kOutput, calls=%fused_computation.22 | convolution fusion | flops 1818427392 | bytes 13565960 | tf_op jit(solution)/shard_map/dot_general | solution.py:81
  528.9 0.0 copy-done.3
  528.9 0.9 copy.30
  (3 shorter events, 0.0 us)
Async XLA Ops:
  7.2 281.0 %copy-start = (bf16[64,3072]{1,0:T(8,128)(2,1)S(1)}, bf16[64,3072]{1,0:T(8,128)(2,1)}, u32[]{:S(2)}) copy-start(bf16[64,3072]{1,0:T(8,128)(2,1)} %param.14) | copy-start | bytes 1179652
  7.2 98.3 %all-gather.11.cloned.1.call-start = ((), (), s32[]{:S(2)}) async-start(), calls=%async_computation.2 | async-start | bytes 10616832 | tf_op jit(solution)/shard_map/all_gather | solution.py:38
  13.4 1.3 copy-start.1
  13.4 131.7 %all-gather.9.cloned.1.call-start = ((), (), s32[]{:S(2)}) async-start(), calls=%async_computation.1 | async-start | bytes 5898240 | tf_op jit(solution)/shard_map/all_gather | solution.py:34
  16.3 189.9 %all-gather.19.cloned.1.call-start = ((), (), s32[]{:S(2)}) async-start(), calls=%async_computation.6 | async-start | bytes 2949120 | tf_op jit(solution)/shard_map/all_gather | solution.py:43
  155.6 101.9 %all-gather.17.cloned.1.call-start = ((), (), s32[]{:S(2)}) async-start(), calls=%async_computation.5 | async-start | bytes 2949120 | tf_op jit(solution)/shard_map/all_gather | solution.py:44
  156.2 169.4 %all-gather.13.cloned.1.call-start = ((), (), s32[]{:S(2)}) async-start(), calls=%async_computation.3 | async-start | bytes 3538944 | tf_op jit(solution)/shard_map/all_gather | solution.py:74
  270.7 7.1 %copy-start.4 = (bf16[64,384]{1,0:T(8,128)(2,1)S(1)}, bf16[64,384]{1,0:T(8,128)(2,1)}, u32[]{:S(2)}) copy-start(bf16[64,384]{1,0:T(8,128)(2,1)} %param.13) | copy-start | bytes 147460
  272.9 14.9 %all-to-all-start = ((bf16[4,192,384]{2,1,0:T(8,128)(2,1)}), bf16[4,192,384]{2,1,0:T(8,128)(2,1)S(1)}, u32[]{:S(2)}, u32[]{:S(2)}) async-start(bf16[4,192,384]{2,1,0:T(8,128)(2,1)} %copy.23), calls=%async_computation | async-start | bytes 1179648 | tf_op jit(solution)/shard_map/all_to_all | solution.py:76
  276.3 179.6 %all-reduce.3.cloned.1.call-start = ((), (), s32[]{:S(2)}) async-start(), calls=%async_computation.7 | async-start | bytes 2359296 | tf_op jit(solution)/shard_map/psum | solution.py:125
  325.5 195.1 %copy-start.2 = (bf16[1,192,3072]{2,1,0:T(8,128)(2,1)S(1)}, bf16[1,192,3072]{2,1,0:T(8,128)(2,1)}, u32[]{:S(2)}) copy-start(bf16[1,192,3072]{2,1,0:T(8,128)(2,1)} %param.9) | copy-start | bytes 3538948
  325.6 195.1 %all-gather.15.cloned.1.call-start = ((), (), s32[]{:S(2)}) async-start(), calls=%async_computation.4 | async-start | bytes 11796480 | tf_op jit(solution)/shard_map/all_gather | solution.py:78
  457.5 71.5 %copy-start.3 = (f32[64,3072]{1,0:T(8,128)S(1)}, f32[64,3072]{1,0:T(8,128)}, u32[]{:S(2)}) copy-start(f32[64,3072]{1,0:T(8,128)} %get-tuple-element.16) | copy-start | bytes 2359300
Sparse Core Ops, SparseCore 0:
  13.5 91.9 all-gather.10
  107.6 37.4 all-gather.8
  155.7 50.4 all-gather.18
  208.2 49.2 all-gather.16
  258.9 34.9 all-gather.12
  325.7 130.1 all-reduce.2
  457.6 63.0 all-gather.14
where the time goes:
time: 537 us
  waiting for transfers between devices  407 us (76%)
  matrix products  53.1 us (10%)
  blocking collectives  40.1 us (7%)
  between operations  17.7 us (3%)
  local copies, waits for them, and re-layouts  13.1 us (2%)
    psum x1, waiting for transfers between devices, shards(): grad_up, down_total = lax.psum((up_part, down_part), ('fsdp', 'uly', 'blk'))  130 us
    all_gather x1, waiting for transfers between devices, shards(): lax.all_gather(query_key_value_weight, 'fsdp', axis=1, tiled=True)  89.1 us
    all_gather x1, waiting for transfers between devices, shards(): lax.all_gather(weight_cols, 'uly', axis=1, tiled=True)  63.2 us
    all_gather x1, waiting for transfers between devices, shards(): lax.all_gather(projected[1], 'blk', axis=0, tiled=True)  48.8 us
    all_gather x1, waiting for transfers between devices, shards(): gathered = lax.all_gather(normed, 'uly', axis=0, tiled=True)  39.6 us
    all_gather x1, waiting for transfers between devices, shards(): lax.all_gather(projected[2], 'blk', axis=0, tiled=True)  35.1 us
    psum x1, blocking collectives, shards(): log_ratio = lax.psum(partial_log, ('uly', 'blk'))  30.2 us
    sub x1, matrix products, shards(): exp_terms = jnp.where(key_ok, jnp.exp(masked - row_max), 0.0)  16.2 us
  transfers between devices with their start and end apart: 8, of which 6 were waited for; matrix products, arithmetic and copies ran while one was open for 8% of the time, Pallas kernels for 0%

commit v1 on v0

v1 whole, which is shorter than its diff:
```python
import math

import jax
import jax.numpy as jnp
from jax import lax
from jax.sharding import PartitionSpec as P

HEAD_SIZE = 128
STEPS = 16


noise_level = 0.7
loss_scale = 4194304.0
rms_eps = 1e-06


def shift(x, axis, by):
    n = lax.axis_size(axis)
    return lax.ppermute(x, axis, [((i + by) % n, i) for i in range(n)])


def swap(x, axis, bit):
    n = lax.axis_size(axis)
    return lax.ppermute(x, axis, [(i ^ bit, i) for i in range(n)])


def bits_of(axis):
    n = lax.axis_size(axis)
    assert n & (n - 1) == 0
    return [1 << i for i in reversed(range(n.bit_length() - 1))]


def xor_gather(x, axis):
    blocks = {0: x}
    for bit in bits_of(axis):
        got = {j ^ bit: swap(v, axis, bit) for j, v in blocks.items()}
        blocks.update(got)
    return [blocks[j] for j in range(lax.axis_size(axis))]


def xor_scatter(blocks, axis):
    held = dict(enumerate(blocks))
    for bit in reversed(bits_of(axis)):
        got = {j ^ bit: swap(v, axis, bit) for j, v in held.items() if j & bit}
        held = {j: held[j] + got[j] for j in got}
    return held[0]


def turn(blocks, me):
    n = len(blocks)
    if n == 1:
        return blocks
    return [
        lax.select_n(
            lax.rem(c - me + n, n), *blocks
        ) if n > 2 else jnp.where(me == c, blocks[0], blocks[1])
        for c in range(n)
    ]


def shards(
    latents,
    sampler_noise,
    query_key_value_weight,
    output_weight,
    adapter_down_map,
    adapter_up_map,
    valid_token_count,
    advantage,
    timestep_index,
):
    fsdp_count = lax.axis_size("fsdp")
    uly_count = lax.axis_size("uly")
    blk_count = lax.axis_size("blk")
    fsdp_id = lax.axis_index("fsdp")
    uly_id = lax.axis_index("uly")
    blk_id = lax.axis_index("blk")
    weights_by_k = {}
    for j in (1, 2, 0):
        own = query_key_value_weight[j]
        weights_by_k[j] = [own] + [shift(own, "fsdp", k) for k in range(1, fsdp_count)]
    out_parts = [output_weight] + [shift(output_weight, "fsdp", k) for k in range(1, fsdp_count)]

    current = latents[0].astype(jnp.float32)
    rows = current.shape[0]
    width = current.shape[1]
    half = width // fsdp_count
    normed = (current * lax.rsqrt(jnp.mean(current * current, -1, keepdims=True) + rms_eps)).astype(
        jnp.bfloat16
    )
    gathered = jnp.concatenate(xor_gather(normed, "uly"), 0)
    halves = [
        lax.dynamic_slice_in_dim(gathered, lax.rem(fsdp_id + k, fsdp_count) * half, half, 1)
        for k in range(fsdp_count)
    ]

    def project(j):
        total = None
        for part, weight in zip(halves, weights_by_k[j]):
            term = jnp.dot(part, weight, preferred_element_type=jnp.float32)
            total = term if total is None else total + term
        return total.astype(jnp.bfloat16)

    def ring(x):
        blocks = [x]
        for _ in range(blk_count - 1):
            blocks.append(shift(blocks[-1], "blk", 1))
        return blocks

    key_blocks = ring(project(1))
    value_blocks = ring(project(2))
    query_rows = project(0)

    limit = valid_token_count[0]
    group_rows = uly_count * rows
    row_index = jnp.arange(group_rows, dtype=jnp.int32)
    row_uly = jnp.bitwise_xor(row_index // rows, uly_id)
    heads_here = query_rows.shape[1] // HEAD_SIZE

    def split(x):
        return x.reshape(x.shape[0], heads_here, HEAD_SIZE)

    query_split = split(query_rows)
    masked = []
    oks = []
    for step in range(blk_count):
        from_blk = lax.rem(blk_id + step, blk_count)
        pos = (row_uly * blk_count + from_blk) * rows + row_index % rows
        ok = (pos < limit)[None, None, :]
        scores = jnp.einsum(
            "qhd,khd->hqk", query_split, split(key_blocks[step]), preferred_element_type=jnp.float32
        ) * (1.0 / math.sqrt(HEAD_SIZE))
        masked.append(jnp.where(ok, scores, -1e30))
        oks.append(ok)
    row_max = jnp.max(masked[0], -1, keepdims=True)
    for m in masked[1:]:
        row_max = jnp.maximum(row_max, jnp.max(m, -1, keepdims=True))
    terms = [jnp.where(ok, jnp.exp(m - row_max), 0.0) for m, ok in zip(masked, oks)]
    total = jnp.sum(terms[0], -1, keepdims=True)
    for t in terms[1:]:
        total = total + jnp.sum(t, -1, keepdims=True)
    attention_output = None
    for t, value in zip(terms, value_blocks):
        part = jnp.einsum(
            "hqk,khd->qhd",
            (t / total).astype(jnp.bfloat16),
            split(value),
            preferred_element_type=jnp.float32,
        )
        attention_output = part if attention_output is None else attention_output + part
    attention_output = attention_output.astype(jnp.bfloat16).reshape(
        group_rows, heads_here * HEAD_SIZE
    )
    contract_product = (((1,), (1,)), ((), ()))
    own_blocks = [
        attention_output[:rows] if j == 0
        else swap(attention_output[j * rows : (j + 1) * rows], "uly", j)
        for j in range(uly_count)
    ]
    own_heads = jnp.concatenate(own_blocks, 1)

    weight_cols = jnp.concatenate(turn(out_parts, fsdp_id), 0)
    weight_full = jnp.concatenate(xor_gather(weight_cols, "uly"), 1)
    down_full = jnp.concatenate(xor_gather(adapter_down_map, "uly"), 1)

    narrow_projection = lax.dot_general(
        own_heads, down_full, contract_product, preferred_element_type=jnp.float32
    ).astype(jnp.bfloat16)
    adapter_result = jnp.dot(narrow_projection, adapter_up_map, preferred_element_type=jnp.float32)
    step_float = timestep_index[0].astype(jnp.float32)
    time_now = 1.0 - step_float / STEPS
    step_size = 1.0 / STEPS
    noise_std = noise_level * jnp.sqrt(time_now / (1.0 - time_now))
    drift_gain = 1.0 + noise_level**2 / 2.0
    ratio_gain = jnp.sqrt(step_size) * drift_gain / noise_std
    noise_f = sampler_noise[0].astype(jnp.float32)
    standard = noise_f + ratio_gain * adapter_result
    tok_pos = (uly_id * blk_count + blk_id) * rows + jnp.arange(rows, dtype=jnp.int32)
    tok_ok = (tok_pos < limit)[:, None]
    valid_len = limit.astype(jnp.float32)
    partial_log = jnp.sum(jnp.where(tok_ok, noise_f * noise_f - standard * standard, 0.0)) / (
        2.0 * valid_len * width
    )
    slots = jnp.where(jnp.arange(uly_count)[:, None] == uly_id, partial_log, 0.0)
    slots = jnp.broadcast_to(slots, (uly_count, HEAD_SIZE))
    slots = sum([swap(slots, "uly", j) for j in range(1, uly_count)], slots)
    by_uly = jnp.sum(slots, 0, keepdims=True)
    lines = jnp.where(jnp.arange(blk_count)[:, None] == blk_id, by_uly, 0.0)
    lines = sum([shift(lines, "blk", k) for k in range(1, blk_count)], lines)
    log_ratio = jnp.sum(lines, 0)[0]
    coef = (
        loss_scale
        * advantage[0]
        * jnp.exp(log_ratio)
        * ratio_gain
        / (fsdp_count * valid_len * width)
    )
    delta_gradient = (jnp.where(tok_ok, standard, 0.0) * coef).astype(jnp.bfloat16)
    first_axis = (((0,), (0,)), ((), ()))
    up_part = lax.dot_general(
        narrow_projection, delta_gradient, first_axis, preferred_element_type=jnp.float32
    )
    narrow_gradient = lax.dot_general(
        delta_gradient, adapter_up_map, contract_product, preferred_element_type=jnp.float32
    ).astype(jnp.bfloat16)
    down_part = lax.dot_general(
        narrow_gradient, own_heads, first_axis, preferred_element_type=jnp.float32
    )

    velocity = lax.dot_general(
        own_heads, weight_full, contract_product, preferred_element_type=jnp.float32
    )
    moved = current - step_size * (
        drift_gain * velocity + noise_level**2 * current / (2.0 * (1.0 - time_now))
    )
    next_latents = (moved + noise_std * jnp.sqrt(step_size) * noise_f).astype(jnp.bfloat16)[None]

    columns = width // uly_count
    local_columns = adapter_down_map.shape[1]
    shares = []
    for j in range(uly_count):
        at = jnp.bitwise_xor(uly_id, j) * columns
        shares.append(
            jnp.concatenate(
                [
                    lax.dynamic_slice_in_dim(up_part, at, columns, 1),
                    down_part[:, j * local_columns : (j + 1) * local_columns],
                ],
                1,
            )
        )
    share = xor_scatter(shares, "uly")
    piece = share.shape[0] // blk_count

    def rows_at(k):
        return lax.dynamic_slice_in_dim(share, lax.rem(blk_id + k, blk_count) * piece, piece, 0)

    mine = rows_at(0)
    for k in range(1, blk_count):
        mine = mine + shift(rows_at(k), "blk", blk_count - k)
    swapped = turn([mine] + [shift(mine, "fsdp", k) for k in range(1, fsdp_count)], fsdp_id)
    mine = sum(swapped[1:], swapped[0])
    whole = jnp.zeros_like(share)
    for k in range(blk_count):
        got = mine if k == 0 else shift(mine, "blk", k)
        whole = lax.dynamic_update_slice_in_dim(
            whole, got, lax.rem(blk_id + k, blk_count) * piece, 0
        )
    grad_down = whole[:, columns:]
    grad_up = jnp.zeros_like(up_part)
    for j, got in enumerate(xor_gather(whole[:, :columns], "uly")):
        grad_up = lax.dynamic_update_slice_in_dim(
            grad_up, got, jnp.bitwise_xor(uly_id, j) * columns, 1
        )
    return (next_latents, jnp.reshape(log_ratio, (1,)), grad_down, grad_up)


def solution(mesh):
    placed = (
        P("fsdp", ("uly", "blk"), None),
        P("fsdp", ("uly", "blk"), None),
        P(None, "fsdp", "uly"),
        P("fsdp", "uly"),
        P(None, "uly"),
        P(),
        P("fsdp"),
        P("fsdp"),
        P(),
    )
    return jax.shard_map(
        shards,
        mesh=mesh,
        in_specs=placed,
        out_specs=(P("fsdp", ("uly", "blk"), None), P("fsdp"), P(None, "uly"), P()),
        check_vma=False,
    )
```

time: 537 us -> 324 us (0.60)
  waiting for transfers between devices: 407 us -> 192 us
  starting transfers between devices: 3.76 us -> 53.4 us
  blocking collectives: 40.1 us -> 0 us
  other arithmetic: 1.68 us -> 19.1 us
  between operations: 17.7 us -> 3.97 us
  matrix products: 53.1 us -> 46.7 us
    all_gather x6 -> x0, waiting for transfers between devices: 276 us -> none  [the longest x1 89.1 us: shards(): lax.all_gather(query_key_value_weight, 'fsdp', axis=1, tiled=True)]
    ppermute x0 -> x41, waiting for transfers between devices: none -> 192 us  [the longest x20 104 us: shift(): return lax.ppermute(x, axis, [((i + by) % n, i) for i in range(n)])]
    psum x1 -> x0, waiting for transfers between devices: 130 us -> none  [shards(): grad_up, down_total = lax.psum((up_part, down_part), ('fsdp', 'uly', 'blk'))]
    ppermute x0 -> x41, starting transfers between devices: none -> 53.4 us  [the longest x20 41.4 us: shift(): return lax.ppermute(x, axis, [((i + by) % n, i) for i in range(n)])]
    psum x1 -> x0, blocking collectives: 30.2 us -> none  [shards(): log_ratio = lax.psum(partial_log, ('uly', 'blk'))]
    sub x1 -> x0, matrix products: 16.2 us -> none  [shards(): exp_terms = jnp.where(key_ok, jnp.exp(masked - row_max), 0.0)]
    all_gather x1 -> x0, blocking collectives: 9.91 us -> none  [shards(): lax.all_gather(adapter_down_map, 'uly', axis=1, tiled=True)]
    reduce_sum x0 -> x3, other arithmetic: none -> 8.81 us  [the longest x1 8.64 us: shards(): total = total + jnp.sum(t, -1, keepdims=True)]
  transfers between devices with their start and end apart: 8 -> 41, of which waited for: 6 -> 23; matrix products, arithmetic and copies ran while one was open for 8% -> 18% of each run, Pallas kernels for 0% -> 0%
where the time goes in v1:
time: 324 us
  waiting for transfers between devices  192 us (59%)
  starting transfers between devices  53.4 us (16%)
  matrix products  46.7 us (14%)
  other arithmetic  19.1 us (6%)
  local copies, waits for them, and re-layouts  8.39 us (3%)
  between operations  3.97 us (1%)
    ppermute x20, waiting for transfers between devices, shift(): return lax.ppermute(x, axis, [((i + by) % n, i) for i in range(n)])  104 us
    ppermute x21, waiting for transfers between devices, swap(): return lax.ppermute(x, axis, [(i ^ bit, i) for i in range(n)])  88.8 us
    ppermute x20, starting transfers between devices, shift(): return lax.ppermute(x, axis, [((i + by) % n, i) for i in range(n)])  41.4 us
    ppermute x21, starting transfers between devices, swap(): return lax.ppermute(x, axis, [(i ^ bit, i) for i in range(n)])  12 us
    dot_general x1, matrix products, shards(): lax.dot_general(own_heads, weight_full, contract_product, preferred_eleme...  10.7 us
    dot_general x4, matrix products, shards(): jnp.einsum('hqk,khd->qhd', (t / total).astype(jnp.bfloat16), split(value)...  9.93 us
    dot_general x6, matrix products, project(): term = jnp.dot(part, weight, preferred_element_type=jnp.float32)  9.74 us
    reduce_sum x1, other arithmetic, shards(): total = total + jnp.sum(t, -1, keepdims=True)  8.64 us
  transfers between devices with their start and end apart: 41, of which 23 were waited for; matrix products, arithmetic and copies ran while one was open for 18% of the time, Pallas kernels for 0%

profile of v1, /device:TPU:0, one launch (start us, length us, event | category | flops | bytes accessed | tf_op | source)
XLA Modules:
  0.0 323.8 jit_solution(9435415262162683702)
XLA Ops:
  0.7 1.7 fusion.46
  2.4 1.6 fusion.47
  4.0 3.0 collective-permute-start.1
  7.0 26.0 %collective-permute-done.1 = bf16[192,3072]{1,0:T(8,128)(2,1)S(1)} collective-permute-done((bf16[192,3072]{1,0:T(8,128)(2,1)S(1)}, bf16[192,3072]{1,0:T(8,128)(2,1)S(1)}, u32[]{:S(2)}, u32[]{:S(2)}) %collective-permute-start.1) | collective-permute-done | bytes 1179680 | tf_op jit(solution)/shard_map/ppermute | solution.py:24
  33.0 1.9 slice_bitcast_fusion
  34.9 1.8 collective-permute-start.5
  36.9 1.7 collective-permute-start.20
  39.5 1.6 collective-permute-start.4
  41.1 2.5 pad_maximum_fusion
  43.6 20.3 %collective-permute-done.5 = bf16[1536,384]{1,0:T(8,128)(2,1)} collective-permute-done((bf16[1536,384]{1,0:T(8,128)(2,1)}, bf16[1536,384]{1,0:T(8,128)(2,1)}, u32[]{:S(2)}, u32[]{:S(2)}) %collective-permute-start.5) | collective-permute-done | bytes 1179680 | tf_op jit(solution)/shard_map/ppermute | solution.py:19
  64.0 1.8 collective-permute-start.15
  65.7 2.5 fusion.49
  68.2 1.2 fusion.74
  69.4 19.8 %collective-permute-done.3 = bf16[1536,384]{1,0:T(8,128)(2,1)} collective-permute-done((bf16[1536,384]{1,0:T(8,128)(2,1)}, bf16[1536,384]{1,0:T(8,128)(2,1)}, u32[]{:S(2)}, u32[]{:S(2)}) %collective-permute-start.3) | collective-permute-done | bytes 1179680 | tf_op jit(solution)/shard_map/ppermute | solution.py:19
  89.2 3.9 %collective-permute-start.6 = (bf16[768,384]{0,1:T(8,128)(2,1)S(1)}, bf16[768,384]{0,1:T(8,128)(2,1)S(1)}, u32[]{:S(2)}, u32[]{:S(2)}) collective-permute-start(bf16[768,384]{0,1:T(8,128)(2,1)S(1)} %fusion.74), channel_id=1, source_target_pairs={{1,0},{2,1},{3,2},{0,3},{5,4},{6,5},{7,6},{4,7},{9,8},{10,9},{11,1... | collective-permute-start | bytes 1769480 | tf_op jit(solution)/shard_map/ppermute | solution.py:19
  93.1 2.5 fusion.53
  95.6 1.2 fusion.80
  96.8 17.6 %collective-permute-done.4 = bf16[1536,384]{1,0:T(8,128)(2,1)S(1)} collective-permute-done((bf16[1536,384]{1,0:T(8,128)(2,1)}, bf16[1536,384]{1,0:T(8,128)(2,1)S(1)}, u32[]{:S(2)}, u32[]{:S(2)}) %collective-permute-start.4) | collective-permute-done | bytes 1179680 | tf_op jit(solution)/shard_map/ppermute | solution.py:19
  114.4 3.9 %collective-permute-start.9 = (bf16[768,384]{0,1:T(8,128)(2,1)S(1)}, bf16[768,384]{0,1:T(8,128)(2,1)S(1)}, u32[]{:S(2)}, u32[]{:S(2)}) collective-permute-start(bf16[768,384]{0,1:T(8,128)(2,1)S(1)} %fusion.80), channel_id=1, source_target_pairs={{1,0},{2,1},{3,2},{0,3},{5,4},{6,5},{7,6},{4,7},{9,8},{10,9},{11,1... | collective-permute-start | bytes 1769480 | tf_op jit(solution)/shard_map/ppermute | solution.py:19
  118.3 1.2 fusion.51
  120.0 1.2 fusion.77
  121.2 10.8 %collective-permute-done.9 = bf16[768,384]{0,1:T(8,128)(2,1)S(1)} collective-permute-done((bf16[768,384]{0,1:T(8,128)(2,1)S(1)}, bf16[768,384]{0,1:T(8,128)(2,1)S(1)}, u32[]{:S(2)}, u32[]{:S(2)}) %collective-permute-start.9) | collective-permute-done | bytes 589856 | tf_op jit(solution)/shard_map/ppermute | solution.py:19
  132.0 4.3 %collective-permute-start.10 = (bf16[768,384]{0,1:T(8,128)(2,1)S(1)}, bf16[768,384]{0,1:T(8,128)(2,1)S(1)}, u32[]{:S(2)}, u32[]{:S(2)}) collective-permute-start(bf16[768,384]{0,1:T(8,128)(2,1)S(1)} %collective-permute-done.9), channel_id=1, source_target_pairs={{1,0},{2,1},{3,2},{0,3},{5,4},{6,5},{7,6},{4,7},{9,8},{10,9},{11,1... | collective-permute-start | bytes 1769480 | tf_op jit(solution)/shard_map/ppermute | solution.py:19
  136.3 1.5 fusion.10
  137.8 6.9 %collective-permute-done.7 = bf16[768,384]{0,1:T(8,128)(2,1)S(1)} collective-permute-done((bf16[768,384]{0,1:T(8,128)(2,1)S(1)}, bf16[768,384]{0,1:T(8,128)(2,1)S(1)}, u32[]{:S(2)}, u32[]{:S(2)}) %collective-permute-start.7) | collective-permute-done | bytes 589856 | tf_op jit(solution)/shard_map/ppermute | solution.py:19
  144.7 4.3 %collective-permute-start.8 = (bf16[768,384]{0,1:T(8,128)(2,1)S(1)}, bf16[768,384]{0,1:T(8,128)(2,1)S(1)}, u32[]{:S(2)}, u32[]{:S(2)}) collective-permute-start(bf16[768,384]{0,1:T(8,128)(2,1)S(1)} %collective-permute-done.7), channel_id=1, source_target_pairs={{1,0},{2,1},{3,2},{0,3},{5,4},{6,5},{7,6},{4,7},{9,8},{10,9},{11,1... | collective-permute-start | bytes 1769480 | tf_op jit(solution)/shard_map/ppermute | solution.py:19
  149.0 1.5 fusion.11
  150.4 6.9 %collective-permute-done.10 = bf16[768,384]{0,1:T(8,128)(2,1)S(1)} collective-permute-done((bf16[768,384]{0,1:T(8,128)(2,1)S(1)}, bf16[768,384]{0,1:T(8,128)(2,1)S(1)}, u32[]{:S(2)}, u32[]{:S(2)}) %collective-permute-start.10) | collective-permute-done | bytes 589856 | tf_op jit(solution)/shard_map/ppermute | solution.py:19
  157.3 4.3 %collective-permute-start.11 = (bf16[768,384]{0,1:T(8,128)(2,1)S(1)}, bf16[768,384]{0,1:T(8,128)(2,1)S(1)}, u32[]{:S(2)}, u32[]{:S(2)}) collective-permute-start(bf16[768,384]{0,1:T(8,128)(2,1)S(1)} %collective-permute-done.10), channel_id=1, source_target_pairs={{1,0},{2,1},{3,2},{0,3},{5,4},{6,5},{7,6},{4,7},{9,8},{10,9},{11,1... | collective-permute-start | bytes 1769480 | tf_op jit(solution)/shard_map/ppermute | solution.py:19
  161.6 1.5 fusion.12
  163.1 6.9 %collective-permute-done.8 = bf16[768,384]{0,1:T(8,128)(2,1)S(1)} collective-permute-done((bf16[768,384]{0,1:T(8,128)(2,1)S(1)}, bf16[768,384]{0,1:T(8,128)(2,1)S(1)}, u32[]{:S(2)}, u32[]{:S(2)}) %collective-permute-start.8) | collective-permute-done | bytes 589856 | tf_op jit(solution)/shard_map/ppermute | solution.py:19
  170.0 1.5 fusion.13
  171.5 8.6 %fusion.15 = (f32[3,768]{1,0:T(4,128)S(1)}, f32[3,768]{1,0:T(4,128)S(1)}, f32[3,768]{1,0:T(4,128)S(1)}, f32[3,768]{1,0:T(4,128)S(1)}) fusion(f32[3,768,768]{1,2,0:T(8,128)S(1)} %get-tuple-element.39, f32[3,768]{1,0:T(4,128)S(1)} %maximum_maximum_fusion, pred[768]{0:T(1024)(128)(4,1)S(1)} %fusion.112, f32[3,768,768]{1,2,0:T(8,128)S(1)} %get-tuple-element.35, ...), kind=kLoop, calls=%fused_computation.27 | loop fusion | flops 35380224 | bytes 28360704 | tf_op jit(solution)/shard_map/reduce_sum | solution.py:141
  180.1 2.5 fusion.39
  182.6 2.5 fusion.63
  185.1 2.5 fusion.62
  187.6 2.5 fusion.83
  190.4 1.6 collective-permute-start.13
  194.1 4.0 %collective-permute-done.13 = bf16[192,384]{0,1:T(8,128)(2,1)S(1)} collective-permute-done((bf16[192,384]{0,1:T(8,128)(2,1)S(1)}, bf16[192,384]{0,1:T(8,128)(2,1)S(1)}, u32[]{:S(2)}, u32[]{:S(2)}) %collective-permute-start.13) | collective-permute-done | bytes 147488 | tf_op jit(solution)/shard_map/ppermute | solution.py:24
  198.1 3.3 %collective-permute-done.14 = bf16[192,384]{0,1:T(8,128)(2,1)S(1)} collective-permute-done((bf16[192,384]{0,1:T(8,128)(2,1)S(1)}, bf16[192,384]{0,1:T(8,128)(2,1)S(1)}, u32[]{:S(2)}, u32[]{:S(2)}) %collective-permute-start.14) | collective-permute-done | bytes 147488 | tf_op jit(solution)/shard_map/ppermute | solution.py:24
  201.4 1.2 convolution_convert_fusion.1
  202.6 4.2 %fusion.45 = (f32[]{:T(128)}, f32[192,3072]{1,0:T(8,128)}) fusion(bf16[1,192,3072]{2,1,0:T(8,128)(2,1)} %param.10, pred[192]{0:T(512)(128)(4,1)S(1)} %add_compare_fusion, bf16[192,64]{0,1:T(8,128)(2,1)S(1)} %convolution_convert_fusion.1, bf16[64,3072]{1,0:T(8,128)(2,1)S(1)} %copy-done, f32[]{:T(128)S(6)} %div.84), kind=kOutput, calls=%fused_computation.51 | convolution fusion | flops 80216064 | bytes 3956936 | tf_op jit(solution)/shard_map/dot_general | solution.py:169
  207.8 1.5 collective-permute-start.23
  209.4 1.5 broadcast_select_fusion.1
  212.5 4.3 %collective-permute-start.25 = (f32[4,128]{1,0:T(4,128)S(1)}, f32[4,128]{1,0:T(4,128)S(1)}, u32[]{:S(2)}, u32[]{:S(2)}) collective-permute-start(f32[4,128]{1,0:T(4,128)S(1)} %broadcast_select_fusion.2), channel_id=1, source_target_pairs={{1,0},{2,1},{3,2},{0,3},{5,4},{6,5},{7,6},{4,7},{9,8},{10,9},{11,1... | collective-permute-start | bytes 6152 | tf_op jit(solution)/shard_map/ppermute | solution.py:19
  217.4 1.7 pad_maximum_fusion.1
  219.7 1.6 collective-permute-done.26
  222.4 2.1 fusion.130
  224.5 2.9 fusion.84
  229.9 48.4 %collective-permute-done.30 = f32[64,1152]{1,0:T(8,128)S(1)} collective-permute-done((f32[64,1152]{1,0:T(8,128)S(1)}, f32[64,1152]{1,0:T(8,128)S(1)}, u32[]{:S(2)}, u32[]{:S(2)}) %collective-permute-start.30) | collective-permute-done | bytes 294944 | tf_op jit(solution)/shard_map/ppermute | solution.py:24
  279.1 2.6 collective-permute-start.31
  281.7 1.2 collective-permute-start.32
  282.8 1.5 collective-permute-start.33
  284.8 1.3 collective-permute-done.31
  286.1 1.9 collective-permute-done.32
  288.9 1.6 collective-permute-start.34
  290.5 2.8 collective-permute-done.34
  293.4 2.6 collective-permute-start.35
  296.6 1.5 collective-permute-done.35
  298.1 3.1 collective-permute-done.36
  301.3 1.2 collective-permute-done.37
  305.4 4.7 %collective-permute-done.39 = f32[64,768]{1,0:T(8,128)S(1)} collective-permute-done((f32[64,768]{1,0:T(8,128)}, f32[64,768]{1,0:T(8,128)S(1)}, u32[]{:S(2)}, u32[]{:S(2)}) %collective-permute-start.39) | collective-permute-done | bytes 196640 | tf_op jit(solution)/shard_map/ppermute | solution.py:24
  310.1 1.6 constant_dynamic-update-slice_fusion.2
  313.1 10.7 %fusion.36 = bf16[1,192,3072]{2,1,0:T(8,128)(2,1)} fusion(bf16[3072,384]{1,0:T(8,128)(2,1)} %collective-permute-done.18, bf16[3072,384]{1,0:T(8,128)(2,1)} %collective-permute-done.17, bf16[3072,384]{1,0:T(8,128)(2,1)} %collective-permute-done.16, bf16[1536,384]{1,0:T(8,128)(2,1)} %copy-done.2, bf16[1536,384]{1,0:T(8,128)(2,1)S(1)} %get-tuple-element.13, ...), kind=kOutput, calls=%fused_computation.42 | convolution fusion | flops 1867972608 | bytes 13565960 | tf_op jit(solution)/shard_map/dot_general | solution.py:210
  (100 shorter events, 15.8 us)
Async XLA Ops:
  0.6 202.0 %copy-start = (bf16[64,3072]{1,0:T(8,128)(2,1)S(1)}, bf16[64,3072]{1,0:T(8,128)(2,1)}, u32[]{:S(2)}) copy-start(bf16[64,3072]{1,0:T(8,128)(2,1)} %param.14) | copy-start | bytes 1179652
  0.6 32.3 %copy-start.3 = (bf16[3,1536,384]{2,1,0:T(8,128)(2,1)S(1)}, bf16[3,1536,384]{2,1,0:T(8,128)(2,1)}, u32[]{:S(2)}) copy-start(bf16[3,1536,384]{2,1,0:T(8,128)(2,1)} %param.11) | copy-start | bytes 10616836
  4.0 29.0 %collective-permute-start.1 = (bf16[192,3072]{1,0:T(8,128)(2,1)S(1)}, bf16[192,3072]{1,0:T(8,128)(2,1)S(1)}, u32[]{:S(2)}, u32[]{:S(2)}) collective-permute-start(bf16[192,3072]{1,0:T(8,128)(2,1)S(1)} %fusion.47), channel_id=1, source_target_pairs={{8,0},{12,4},{0,8},{4,12},{9,1},{13,5},{1,9},{5,13},{10,2},{14,6},... | collective-permute-start | bytes 3538952 | tf_op jit(solution)/shard_map/ppermute | solution.py:24
  7.0 32.4 %collective-permute-start = (bf16[192,3072]{1,0:T(8,128)(2,1)S(1)}, bf16[192,3072]{1,0:T(8,128)(2,1)}, u32[]{:S(2)}, u32[]{:S(2)}) collective-permute-start(bf16[192,3072]{1,0:T(8,128)(2,1)S(1)} %fusion.47), channel_id=1, source_target_pairs={{4,0},{0,4},{12,8},{8,12},{5,1},{1,5},{13,9},{9,13},{6,2},{2,6},{1... | collective-permute-start | bytes 3538952 | tf_op jit(solution)/shard_map/ppermute | solution.py:24
  33.0 6.5 %collective-permute-start.2 = (bf16[192,3072]{1,0:T(8,128)(2,1)S(1)}, bf16[192,3072]{1,0:T(8,128)(2,1)}, u32[]{:S(2)}, u32[]{:S(2)}) collective-permute-start(bf16[192,3072]{1,0:T(8,128)(2,1)S(1)} %collective-permute-done.1), channel_id=1, source_target_pairs={{4,0},{0,4},{12,8},{8,12},{5,1},{1,5},{13,9},{9,13},{6,2},{2,6},{1... | collective-permute-start | bytes 3538952 | tf_op jit(solution)/shard_map/ppermute | solution.py:24
  34.9 29.1 %collective-permute-start.5 = (bf16[1536,384]{1,0:T(8,128)(2,1)}, bf16[1536,384]{1,0:T(8,128)(2,1)}, u32[]{:S(2)}, u32[]{:S(2)}) collective-permute-start(bf16[1536,384]{1,0:T(8,128)(2,1)} %get-tuple-element.10), channel_id=1, source_target_pairs={{16,0},{0,16},{17,1},{1,17},{18,2},{2,18},{19,3},{3,19},{20,4},{4,... | collective-permute-start | bytes 3538952 | tf_op jit(solution)/shard_map/ppermute | solution.py:19
  36.6 52.6 %collective-permute-start.3 = (bf16[1536,384]{1,0:T(8,128)(2,1)}, bf16[1536,384]{1,0:T(8,128)(2,1)}, u32[]{:S(2)}, u32[]{:S(2)}) collective-permute-start(bf16[1536,384]{1,0:T(8,128)(2,1)} %get-tuple-element.11), channel_id=1, source_target_pairs={{16,0},{0,16},{17,1},{1,17},{18,2},{2,18},{19,3},{3,19},{20,4},{4,... | collective-permute-start | bytes 3538952 | tf_op jit(solution)/shard_map/ppermute | solution.py:19
  36.9 155.0 %collective-permute-start.20 = (bf16[64,384]{1,0:T(8,128)(2,1)}, bf16[64,384]{1,0:T(8,128)(2,1)}, u32[]{:S(2)}, u32[]{:S(2)}) collective-permute-start(bf16[64,384]{1,0:T(8,128)(2,1)} %param.13), channel_id=1, source_target_pairs={{8,0},{12,4},{0,8},{4,12},{9,1},{13,5},{1,9},{5,13},{10,2},{14,6},... | collective-permute-start | bytes 147464 | tf_op jit(solution)/shard_map/ppermute | solution.py:24
  39.4 152.8 %collective-permute-start.19 = (bf16[64,384]{1,0:T(8,128)(2,1)}, bf16[64,384]{1,0:T(8,128)(2,1)}, u32[]{:S(2)}, u32[]{:S(2)}) collective-permute-start(bf16[64,384]{1,0:T(8,128)(2,1)} %param.13), channel_id=1, source_target_pairs={{4,0},{0,4},{12,8},{8,12},{5,1},{1,5},{13,9},{9,13},{6,2},{2,6},{1... | collective-permute-start | bytes 147464 | tf_op jit(solution)/shard_map/ppermute | solution.py:24
  39.5 74.9 %collective-permute-start.4 = (bf16[1536,384]{1,0:T(8,128)(2,1)}, bf16[1536,384]{1,0:T(8,128)(2,1)S(1)}, u32[]{:S(2)}, u32[]{:S(2)}) collective-permute-start(bf16[1536,384]{1,0:T(8,128)(2,1)} %get-tuple-element.12), channel_id=1, source_target_pairs={{16,0},{0,16},{17,1},{1,17},{18,2},{2,18},{19,3},{3,19},{20,4},{4,... | collective-permute-start | bytes 3538952 | tf_op jit(solution)/shard_map/ppermute | solution.py:19
  43.6 24.6 %copy-start.4 = (bf16[3,1536,384]{2,1,0:T(8,128)(2,1)S(1)}, bf16[3,1536,384]{2,1,0:T(8,128)(2,1)}, u32[]{:S(2)}) copy-start(bf16[3,1536,384]{2,1,0:T(8,128)(2,1)} %param.11) | copy-start | bytes 10616836
  64.0 145.5 %collective-permute-start.15 = (bf16[1536,384]{1,0:T(8,128)(2,1)}, bf16[1536,384]{1,0:T(8,128)(2,1)S(1)}, u32[]{:S(2)}, u32[]{:S(2)}) collective-permute-start(bf16[1536,384]{1,0:T(8,128)(2,1)} %param.12), channel_id=1, source_target_pairs={{16,0},{0,16},{17,1},{1,17},{18,2},{2,18},{19,3},{3,19},{20,4},{4,... | collective-permute-start | bytes 3538952 | tf_op jit(solution)/shard_map/ppermute | solution.py:19
  89.2 30.2 %collective-permute-start.6 = (bf16[768,384]{0,1:T(8,128)(2,1)S(1)}, bf16[768,384]{0,1:T(8,128)(2,1)S(1)}, u32[]{:S(2)}, u32[]{:S(2)}) collective-permute-start(bf16[768,384]{0,1:T(8,128)(2,1)S(1)} %fusion.74), channel_id=1, source_target_pairs={{1,0},{2,1},{3,2},{0,3},{5,4},{6,5},{7,6},{4,7},{9,8},{10,9},{11,1... | collective-permute-start | bytes 1769480 | tf_op jit(solution)/shard_map/ppermute | solution.py:19
  114.4 17.6 %collective-permute-start.9 = (bf16[768,384]{0,1:T(8,128)(2,1)S(1)}, bf16[768,384]{0,1:T(8,128)(2,1)S(1)}, u32[]{:S(2)}, u32[]{:S(2)}) collective-permute-start(bf16[768,384]{0,1:T(8,128)(2,1)S(1)} %fusion.80), channel_id=1, source_target_pairs={{1,0},{2,1},{3,2},{0,3},{5,4},{6,5},{7,6},{4,7},{9,8},{10,9},{11,1... | collective-permute-start | bytes 1769480 | tf_op jit(solution)/shard_map/ppermute | solution.py:19
  119.5 25.2 %collective-permute-start.7 = (bf16[768,384]{0,1:T(8,128)(2,1)S(1)}, bf16[768,384]{0,1:T(8,128)(2,1)S(1)}, u32[]{:S(2)}, u32[]{:S(2)}) collective-permute-start(bf16[768,384]{0,1:T(8,128)(2,1)S(1)} %collective-permute-done.6), channel_id=1, source_target_pairs={{1,0},{2,1},{3,2},{0,3},{5,4},{6,5},{7,6},{4,7},{9,8},{10,9},{11,1... | collective-permute-start | bytes 1769480 | tf_op jit(solution)/shard_map/ppermute | solution.py:19
  132.0 25.3 %collective-permute-start.10 = (bf16[768,384]{0,1:T(8,128)(2,1)S(1)}, bf16[768,384]{0,1:T(8,128)(2,1)S(1)}, u32[]{:S(2)}, u32[]{:S(2)}) collective-permute-start(bf16[768,384]{0,1:T(8,128)(2,1)S(1)} %collective-permute-done.9), channel_id=1, source_target_pairs={{1,0},{2,1},{3,2},{0,3},{5,4},{6,5},{7,6},{4,7},{9,8},{10,9},{11,1... | collective-permute-start | bytes 1769480 | tf_op jit(solution)/shard_map/ppermute | solution.py:19
  144.7 25.3 %collective-permute-start.8 = (bf16[768,384]{0,1:T(8,128)(2,1)S(1)}, bf16[768,384]{0,1:T(8,128)(2,1)S(1)}, u32[]{:S(2)}, u32[]{:S(2)}) collective-permute-start(bf16[768,384]{0,1:T(8,128)(2,1)S(1)} %collective-permute-done.7), channel_id=1, source_target_pairs={{1,0},{2,1},{3,2},{0,3},{5,4},{6,5},{7,6},{4,7},{9,8},{10,9},{11,1... | collective-permute-start | bytes 1769480 | tf_op jit(solution)/shard_map/ppermute | solution.py:19
  157.3 30.2 %collective-permute-start.11 = (bf16[768,384]{0,1:T(8,128)(2,1)S(1)}, bf16[768,384]{0,1:T(8,128)(2,1)S(1)}, u32[]{:S(2)}, u32[]{:S(2)}) collective-permute-start(bf16[768,384]{0,1:T(8,128)(2,1)S(1)} %collective-permute-done.10), channel_id=1, source_target_pairs={{1,0},{2,1},{3,2},{0,3},{5,4},{6,5},{7,6},{4,7},{9,8},{10,9},{11,1... | collective-permute-start | bytes 1769480 | tf_op jit(solution)/shard_map/ppermute | solution.py:19
  190.3 3.8 %collective-permute-start.12 = (bf16[192,384]{0,1:T(8,128)(2,1)S(1)}, bf16[192,384]{0,1:T(8,128)(2,1)S(1)}, u32[]{:S(2)}, u32[]{:S(2)}) collective-permute-start(bf16[192,384]{0,1:T(8,128)(2,1)S(1)} %bitcast.78), channel_id=1, source_target_pairs={{4,0},{0,4},{12,8},{8,12},{5,1},{1,5},{13,9},{9,13},{6,2},{2,6},{1... | collective-permute-start | bytes 442376 | tf_op jit(solution)/shard_map/ppermute | solution.py:24
  190.4 7.8 %collective-permute-start.13 = (bf16[192,384]{0,1:T(8,128)(2,1)S(1)}, bf16[192,384]{0,1:T(8,128)(2,1)S(1)}, u32[]{:S(2)}, u32[]{:S(2)}) collective-permute-start(bf16[192,384]{0,1:T(8,128)(2,1)S(1)} %bitcast.77), channel_id=1, source_target_pairs={{8,0},{12,4},{0,8},{4,12},{9,1},{13,5},{1,9},{5,13},{10,2},{14,6},... | collective-permute-start | bytes 442376 | tf_op jit(solution)/shard_map/ppermute | solution.py:24
  191.9 9.5 %collective-permute-start.14 = (bf16[192,384]{0,1:T(8,128)(2,1)S(1)}, bf16[192,384]{0,1:T(8,128)(2,1)S(1)}, u32[]{:S(2)}, u32[]{:S(2)}) collective-permute-start(bf16[192,384]{0,1:T(8,128)(2,1)S(1)} %bitcast.76), channel_id=1, source_target_pairs={{12,0},{8,4},{4,8},{0,12},{13,1},{9,5},{5,9},{1,13},{14,2},{10,6},... | collective-permute-start | bytes 442376 | tf_op jit(solution)/shard_map/ppermute | solution.py:24
  192.2 1.9 collective-permute-start.21
  194.1 12.7 %copy-start.6 = (bf16[192,384]{0,1:T(8,128)(2,1)}, bf16[192,384]{0,1:T(8,128)(2,1)S(1)}, u32[]{:S(2)}) copy-start(bf16[192,384]{0,1:T(8,128)(2,1)S(1)} %collective-permute-done.12) | copy-start | bytes 442372
  198.1 8.7 %copy-start.8 = (bf16[192,384]{0,1:T(8,128)(2,1)}, bf16[192,384]{0,1:T(8,128)(2,1)S(1)}, u32[]{:S(2)}) copy-start(bf16[192,384]{0,1:T(8,128)(2,1)S(1)} %collective-permute-done.13) | copy-start | bytes 442372
  201.4 5.4 %copy-start.10 = (bf16[192,384]{0,1:T(8,128)(2,1)}, bf16[192,384]{0,1:T(8,128)(2,1)S(1)}, u32[]{:S(2)}) copy-start(bf16[192,384]{0,1:T(8,128)(2,1)S(1)} %collective-permute-done.14) | copy-start | bytes 442372
  207.5 3.4 %collective-permute-start.22 = (f32[4,128]{1,0:T(4,128)S(1)}, f32[4,128]{1,0:T(4,128)S(1)}, u32[]{:S(2)}, u32[]{:S(2)}) collective-permute-start(f32[4,128]{1,0:T(4,128)S(1)} %broadcast_in_dim.135), channel_id=1, source_target_pairs={{4,0},{0,4},{12,8},{8,12},{5,1},{1,5},{13,9},{9,13},{6,2},{2,6},{1... | collective-permute-start | bytes 6152 | tf_op jit(solution)/shard_map/ppermute | solution.py:24
  207.8 3.6 %collective-permute-start.23 = (f32[4,128]{1,0:T(4,128)S(1)}, f32[4,128]{1,0:T(4,128)S(1)}, u32[]{:S(2)}, u32[]{:S(2)}) collective-permute-start(f32[4,128]{1,0:T(4,128)S(1)} %broadcast_in_dim.135), channel_id=1, source_target_pairs={{8,0},{12,4},{0,8},{4,12},{9,1},{13,5},{1,9},{5,13},{10,2},{14,6},... | collective-permute-start | bytes 6152 | tf_op jit(solution)/shard_map/ppermute | solution.py:24
  209.3 3.0 collective-permute-start.24
  210.9 8.2 %copy-start.2 = (bf16[1536,384]{1,0:T(8,128)(2,1)}, bf16[1536,384]{1,0:T(8,128)(2,1)S(1)}, u32[]{:S(2)}) copy-start(bf16[1536,384]{1,0:T(8,128)(2,1)S(1)} %get-tuple-element.14) | copy-start | bytes 3538948
  212.5 7.2 %collective-permute-start.25 = (f32[4,128]{1,0:T(4,128)S(1)}, f32[4,128]{1,0:T(4,128)S(1)}, u32[]{:S(2)}, u32[]{:S(2)}) collective-permute-start(f32[4,128]{1,0:T(4,128)S(1)} %broadcast_select_fusion.2), channel_id=1, source_target_pairs={{1,0},{2,1},{3,2},{0,3},{5,4},{6,5},{7,6},{4,7},{9,8},{10,9},{11,1... | collective-permute-start | bytes 6152 | tf_op jit(solution)/shard_map/ppermute | solution.py:19
  216.8 4.5 %collective-permute-start.26 = (f32[4,128]{1,0:T(4,128)S(1)}, f32[4,128]{1,0:T(4,128)S(1)}, u32[]{:S(2)}, u32[]{:S(2)}) collective-permute-start(f32[4,128]{1,0:T(4,128)S(1)} %broadcast_select_fusion.2), channel_id=1, source_target_pairs={{2,0},{3,1},{0,2},{1,3},{6,4},{7,5},{4,6},{5,7},{10,8},{11,9},{8,1... | collective-permute-start | bytes 6152 | tf_op jit(solution)/shard_map/ppermute | solution.py:19
  216.8 5.4 %collective-permute-start.27 = (f32[4,128]{1,0:T(4,128)S(1)}, f32[4,128]{1,0:T(4,128)S(1)}, u32[]{:S(2)}, u32[]{:S(2)}) collective-permute-start(f32[4,128]{1,0:T(4,128)S(1)} %broadcast_select_fusion.2), channel_id=1, source_target_pairs={{3,0},{0,1},{1,2},{2,3},{7,4},{4,5},{5,6},{6,7},{11,8},{8,9},{9,10... | collective-permute-start | bytes 6152 | tf_op jit(solution)/shard_map/ppermute | solution.py:19
  219.1 5.4 %copy-start.7 = (bf16[192,384]{0,1:T(8,128)(2,1)S(1)}, bf16[192,384]{0,1:T(8,128)(2,1)}, u32[]{:S(2)}) copy-start(bf16[192,384]{0,1:T(8,128)(2,1)} %copy-done.6) | copy-start | bytes 442372
  219.1 5.4 %copy-start.9 = (bf16[192,384]{0,1:T(8,128)(2,1)S(1)}, bf16[192,384]{0,1:T(8,128)(2,1)}, u32[]{:S(2)}) copy-start(bf16[192,384]{0,1:T(8,128)(2,1)} %copy-done.8) | copy-start | bytes 442372
  219.1 65.2 %collective-permute-start.17 = (bf16[3072,384]{1,0:T(8,128)(2,1)}, bf16[3072,384]{1,0:T(8,128)(2,1)}, u32[]{:S(2)}, u32[]{:S(2)}) collective-permute-start(bf16[3072,384]{1,0:T(8,128)(2,1)} %pad_maximum_fusion.1), channel_id=1, source_target_pairs={{8,0},{12,4},{0,8},{4,12},{9,1},{13,5},{1,9},{5,13},{10,2},{14,6},... | collective-permute-start | bytes 7077896 | tf_op jit(solution)/shard_map/ppermute | solution.py:24
  222.3 5.2 %copy-start.5 = (f32[128]{0:T(128)}, f32[128]{0:T(128)S(1)}, u32[]{:S(2)}) copy-start(f32[128]{0:T(128)S(1)} %add_reduce_fusion) | copy-start | bytes 1540
  227.6 1.6 collective-permute-start.29
  227.7 2.2 collective-permute-start.28
  229.3 49.1 %collective-permute-start.30 = (f32[64,1152]{1,0:T(8,128)S(1)}, f32[64,1152]{1,0:T(8,128)S(1)}, u32[]{:S(2)}, u32[]{:S(2)}) collective-permute-start(f32[64,1152]{1,0:T(8,128)S(1)} %maximum_add_fusion.1), channel_id=1, source_target_pairs={{8,0},{12,4},{0,8},{4,12},{9,1},{13,5},{1,9},{5,13},{10,2},{14,6},... | collective-permute-start | bytes 884744 | tf_op jit(solution)/shard_map/ppermute | solution.py:24
  278.4 34.7 %copy-start.1 = (bf16[1,192,3072]{2,1,0:T(8,128)(2,1)S(1)}, bf16[1,192,3072]{2,1,0:T(8,128)(2,1)}, u32[]{:S(2)}) copy-start(bf16[1,192,3072]{2,1,0:T(8,128)(2,1)} %param.9) | copy-start | bytes 3538948
  279.1 7.0 %collective-permute-start.31 = (f32[16,1152]{1,0:T(8,128)}, f32[16,1152]{1,0:T(8,128)S(1)}, u32[]{:S(2)}, u32[]{:S(2)}) collective-permute-start(f32[16,1152]{1,0:T(8,128)} %get-tuple-element.29), channel_id=1, source_target_pairs={{3,0},{0,1},{1,2},{2,3},{7,4},{4,5},{5,6},{6,7},{11,8},{8,9},{9,10... | collective-permute-start | bytes 221192 | tf_op jit(solution)/shard_map/ppermute | solution.py:19
  281.7 6.3 %collective-permute-start.32 = (f32[16,1152]{1,0:T(8,128)S(1)}, f32[16,1152]{1,0:T(8,128)S(1)}, u32[]{:S(2)}, u32[]{:S(2)}) collective-permute-start(f32[16,1152]{1,0:T(8,128)S(1)} %get-tuple-element.31), channel_id=1, source_target_pairs={{2,0},{3,1},{0,2},{1,3},{6,4},{7,5},{4,6},{5,7},{10,8},{11,9},{8,1... | collective-permute-start | bytes 221192 | tf_op jit(solution)/shard_map/ppermute | solution.py:19
  282.8 5.1 %collective-permute-start.33 = (f32[16,1152]{1,0:T(8,128)S(1)}, f32[16,1152]{1,0:T(8,128)}, u32[]{:S(2)}, u32[]{:S(2)}) collective-permute-start(f32[16,1152]{1,0:T(8,128)S(1)} %get-tuple-element.30), channel_id=1, source_target_pairs={{1,0},{2,1},{3,2},{0,3},{5,4},{6,5},{7,6},{4,7},{9,8},{10,9},{11,1... | collective-permute-start | bytes 221192 | tf_op jit(solution)/shard_map/ppermute | solution.py:19
  284.3 28.8 %collective-permute-start.16 = (bf16[3072,384]{1,0:T(8,128)(2,1)}, bf16[3072,384]{1,0:T(8,128)(2,1)}, u32[]{:S(2)}, u32[]{:S(2)}) collective-permute-start(bf16[3072,384]{1,0:T(8,128)(2,1)} %pad_maximum_fusion.1), channel_id=1, source_target_pairs={{4,0},{0,4},{12,8},{8,12},{5,1},{1,5},{13,9},{9,13},{6,2},{2,6},{1... | collective-permute-start | bytes 7077896 | tf_op jit(solution)/shard_map/ppermute | solution.py:24
  284.3 28.8 %collective-permute-start.18 = (bf16[3072,384]{1,0:T(8,128)(2,1)}, bf16[3072,384]{1,0:T(8,128)(2,1)}, u32[]{:S(2)}, u32[]{:S(2)}) collective-permute-start(bf16[3072,384]{1,0:T(8,128)(2,1)} %collective-permute-done.17), channel_id=1, source_target_pairs={{4,0},{0,4},{12,8},{8,12},{5,1},{1,5},{13,9},{9,13},{6,2},{2,6},{1... | collective-permute-start | bytes 7077896 | tf_op jit(solution)/shard_map/ppermute | solution.py:24
  288.9 4.4 %collective-permute-start.34 = (f32[16,1152]{1,0:T(8,128)S(1)}, f32[16,1152]{1,0:T(8,128)S(1)}, u32[]{:S(2)}, u32[]{:S(2)}) collective-permute-start(f32[16,1152]{1,0:T(8,128)S(1)} %add_add_fusion), channel_id=1, source_target_pairs={{16,0},{0,16},{17,1},{1,17},{18,2},{2,18},{19,3},{3,19},{20,4},{4,... | collective-permute-start | bytes 221192 | tf_op jit(solution)/shard_map/ppermute | solution.py:19
  293.4 4.8 %collective-permute-start.35 = (f32[16,1152]{1,0:T(8,128)S(1)}, f32[16,1152]{1,0:T(8,128)S(1)}, u32[]{:S(2)}, u32[]{:S(2)}) collective-permute-start(f32[16,1152]{1,0:T(8,128)S(1)} %get-tuple-element.9), channel_id=1, source_target_pairs={{1,0},{2,1},{3,2},{0,3},{5,4},{6,5},{7,6},{4,7},{9,8},{10,9},{11,1... | collective-permute-start | bytes 221192 | tf_op jit(solution)/shard_map/ppermute | solution.py:19
  296.0 5.3 %collective-permute-start.36 = (f32[16,1152]{1,0:T(8,128)S(1)}, f32[16,1152]{1,0:T(8,128)S(1)}, u32[]{:S(2)}, u32[]{:S(2)}) collective-permute-start(f32[16,1152]{1,0:T(8,128)S(1)} %get-tuple-element.9), channel_id=1, source_target_pairs={{2,0},{3,1},{0,2},{1,3},{6,4},{7,5},{4,6},{5,7},{10,8},{11,9},{8,1... | collective-permute-start | bytes 221192 | tf_op jit(solution)/shard_map/ppermute | solution.py:19
  296.3 6.2 %collective-permute-start.37 = (f32[16,1152]{1,0:T(8,128)S(1)}, f32[16,1152]{1,0:T(8,128)S(1)}, u32[]{:S(2)}, u32[]{:S(2)}) collective-permute-start(f32[16,1152]{1,0:T(8,128)S(1)} %get-tuple-element.9), channel_id=1, source_target_pairs={{3,0},{0,1},{1,2},{2,3},{7,4},{4,5},{5,6},{6,7},{11,8},{8,9},{9,10... | collective-permute-start | bytes 221192 | tf_op jit(solution)/shard_map/ppermute | solution.py:19
  304.2 5.9 %collective-permute-start.39 = (f32[64,768]{1,0:T(8,128)}, f32[64,768]{1,0:T(8,128)S(1)}, u32[]{:S(2)}, u32[]{:S(2)}) collective-permute-start(f32[64,768]{1,0:T(8,128)} %get-tuple-element.27), channel_id=1, source_target_pairs={{8,0},{12,4},{0,8},{4,12},{9,1},{13,5},{1,9},{5,13},{10,2},{14,6},... | collective-permute-start | bytes 589832 | tf_op jit(solution)/shard_map/ppermute | solution.py:24
  304.8 5.3 %collective-permute-start.38 = (f32[64,768]{1,0:T(8,128)}, f32[64,768]{1,0:T(8,128)}, u32[]{:S(2)}, u32[]{:S(2)}) collective-permute-start(f32[64,768]{1,0:T(8,128)} %get-tuple-element.27), channel_id=1, source_target_pairs={{4,0},{0,4},{12,8},{8,12},{5,1},{1,5},{13,9},{9,13},{6,2},{2,6},{1... | collective-permute-start | bytes 589832 | tf_op jit(solution)/shard_map/ppermute | solution.py:24
  310.1 2.3 collective-permute-start.40
